TPU v7x, 32 devices: a whole 2x2x4 slice. The times are simulated.
32 devices in a mesh: ctx: 8 (over y, x, core), tp: 4 (over z).
Axes of the slice: x: 2, y: 2, z: 4, core: 2. Of those that a mesh axis runs over, the one named last changes fastest.
Arguments:
- queries: bfloat16 [2048, 4096], P('ctx', 'tp'), may hold values from -12 to 12, as said below
- key_rows: bfloat16 [2048, 1024], P('ctx', 'tp'), may hold values from -12 to 12, as said below
- value_rows: bfloat16 [2048, 1024], P('ctx', 'tp'), may hold values from -6 to 6
- segments: int32 [2048], replicated, may hold values from 0 to 15, never falling along the last dimension, each value on 1 to 1024 neighbouring positions
- owner_ids: int32 [2048, 1], P('ctx'), may hold values from 0 to 3; in each aligned block of 256 rows (0 to 255, 256 to 511, ...) at most 64 rows name the same one
- out_proj: bfloat16 [4096, 8192], P('tp'), may hold values from -0.09375 to 0.09375
- residual: bfloat16 [2048, 8192], P(('ctx', 'tp')), may hold values from -4 to 4
- norm_gain: float32 [8192], replicated, may hold values from 0.5 to 1.5
Outputs:
- hidden_out: bfloat16 [2048, 8192], P(('ctx', 'tp'))
- normed: bfloat16 [2048, 8192], P(('ctx', 'tp'))
Inputs may be any that keep to these rules, and one draw needn't show every extreme that they name: `segments`: never falling along the tokens; every document has 1 to 1024 tokens and one has exactly 1024. `owner_ids`: among the rows of one device's token block no owner is named more than 64 times; some owner is named exactly 64 times in some block. `queries`: Real-valued entries. `key_rows`: Real-valued entries.
All inputs are finite; a program needn't handle non-finite values.
Results may differ from a plain program's by a relative error of at most 0.01.
Values may be sent and summed in bfloat16 or wider, within the bound.
A program may use at most 128 MiB of HBM per device.

v0:
```python
import math

import jax
import jax.numpy as jnp
from jax import lax
from jax.sharding import PartitionSpec as P

HEADS = 32
KV_HEADS = 8
HEAD_DIM = 128


def slot_sources(owners, row_rank, owner_here, slot_count):
    token_count = owners.shape[0]
    slot_numbers = jnp.arange(slot_count, dtype=jnp.int32)[:, None]
    matches = ((owners[None, :] == owner_here) & (row_rank[None, :] == slot_numbers)).astype(
        jnp.int32
    )
    token_index = jnp.sum(matches * jnp.arange(token_count, dtype=jnp.int32)[None, :], axis=1)
    filled = jnp.sum(matches, axis=1) > 0
    return (token_index, filled)


def on_device(queries, key_rows, value_rows, segments, owner_ids, out_proj, residual, norm_gain):
    rows_here = queries.shape[0]
    kv_local = key_rows.shape[1] // HEAD_DIM
    group_size = HEADS // KV_HEADS
    score_scale = 1.0 / math.sqrt(HEAD_DIM)
    my_start = lax.axis_index("ctx") * rows_here
    query_heads = queries.reshape(rows_here, kv_local, group_size, HEAD_DIM)
    query_pos = my_start + jnp.arange(rows_here, dtype=jnp.int32)
    query_seg = lax.dynamic_slice_in_dim(segments, my_start, rows_here, 0)
    start_state = (
        jnp.full((kv_local, group_size, rows_here), -1e30, jnp.float32),
        jnp.zeros((kv_local, group_size, rows_here), jnp.float32),
        jnp.zeros((kv_local, group_size, rows_here, HEAD_DIM), jnp.float32),
    )
    carried = start_state
    key_piece = lax.all_gather(key_rows, "ctx", axis=0, tiled=True)
    value_piece = lax.all_gather(value_rows, "ctx", axis=0, tiled=True)
    piece_rows = key_piece.shape[0]
    key_width = 512
    block_count = piece_rows // key_width
    key_blocks = key_piece.reshape(block_count, key_width, kv_local, HEAD_DIM)
    value_blocks = value_piece.reshape(block_count, key_width, kv_local, HEAD_DIM)

    def update(states, block_item):
        block_index, key_block, value_block = block_item
        key_start = block_index * key_width
        key_seg = lax.dynamic_slice_in_dim(segments, key_start, key_width, 0)
        key_pos = key_start + jnp.arange(key_width, dtype=jnp.int32)
        allowed = (query_seg[:, None] == key_seg[None, :]) & (
            key_pos[None, :] <= query_pos[:, None]
        )
        running_max, totals, weighted = states
        scores = (
            jnp.einsum("tkgd,skd->kgts", query_heads, key_block, preferred_element_type=jnp.float32)
            * score_scale
        )
        scores = jnp.where(allowed, scores, -1e30)
        new_max = jnp.maximum(running_max, jnp.max(scores, axis=-1))
        exponent = jnp.where(allowed, jnp.exp(scores - new_max[..., None]), 0.0)
        factor = jnp.exp(running_max - new_max)
        totals = totals * factor + jnp.sum(exponent, axis=-1)
        weighted = weighted * factor[..., None] + jnp.einsum(
            "kgts,skd->kgtd",
            exponent.astype(jnp.bfloat16),
            value_block,
            preferred_element_type=jnp.float32,
        )
        states = (new_max, totals, weighted)
        return (states, None)

    carried, _ = lax.scan(
        update, carried, (jnp.arange(block_count, dtype=jnp.int32), key_blocks, value_blocks)
    )
    running_max, totals, weighted = carried
    mixed_heads = weighted / totals[..., None]
    attended = jnp.transpose(mixed_heads, (2, 0, 1, 3)).reshape(rows_here, -1).astype(jnp.bfloat16)
    partial_rows = jnp.dot(attended, out_proj, preferred_element_type=jnp.float32).astype(
        jnp.bfloat16
    )
    slot_count = residual.shape[0]
    owner_count = lax.axis_size("tp")
    owner_here = lax.axis_index("tp")
    owners = owner_ids[:, 0]
    onehot = (owners[:, None] == jnp.arange(owner_count, dtype=jnp.int32)[None, :]).astype(
        jnp.int32
    )
    before = jnp.cumsum(onehot, axis=0) - onehot
    row_rank = jnp.sum(before * onehot, axis=1)
    summed = lax.psum(partial_rows.astype(jnp.float32).astype(jnp.bfloat16), "tp").astype(
        jnp.float32
    )
    token_index, filled = slot_sources(owners, row_rank, owner_here, slot_count)
    owned_rows = jnp.where(filled[:, None], jnp.take(summed, token_index, axis=0), 0.0)
    hidden_sum = residual.astype(jnp.float32) + owned_rows
    mean_square = jnp.mean(hidden_sum * hidden_sum, axis=-1, keepdims=True)
    normed = hidden_sum * lax.rsqrt(mean_square + 1e-05) * norm_gain
    return (hidden_sum.astype(jnp.bfloat16), normed.astype(jnp.bfloat16))


def solution(mesh):
    placed = (
        P("ctx", "tp"),
        P("ctx", "tp"),
        P("ctx", "tp"),
        P(),
        P("ctx", None),
        P("tp", None),
        P(("ctx", "tp"), None),
        P(),
    )
    return jax.shard_map(
        on_device,
        mesh=mesh,
        in_specs=placed,
        out_specs=(P(("ctx", "tp"), None), P(("ctx", "tp"), None)),
        check_vma=False,
    )
```

profile of v0, /device:TPU:20, one launch (start us, length us, event | category | flops | bytes accessed | tf_op | source)
XLA Modules:
  0.0 299.7 jit_solution(16484836976000150615)
XLA Ops:
  8.7 1.2 copy.24
  11.0 23.4 %all-gather.3.cloned.1.call-done = bf16[2048,256]{1,0:T(8,128)(2,1)} async-done(((bf16[256,256]{1,0:T(8,128)(2,1)}), bf16[2048,256]{1,0:T(8,128)(2,1)}) %all-gather.3.cloned.1.call-update) | async-done | bytes 1048592 | tf_op jit(solution)/shard_map/all_gather | solution.py:39
  34.4 1.3 reshape.82
  35.7 24.1 %all-gather.5.cloned.1.call-done = bf16[2048,256]{1,0:T(8,128)(2,1)} async-done(((bf16[256,256]{1,0:T(8,128)(2,1)}), bf16[2048,256]{1,0:T(8,128)(2,1)}) %all-gather.5.cloned.1.call-update) | async-done | bytes 1048592 | tf_op jit(solution)/shard_map/all_gather | solution.py:40
  59.8 1.3 reshape.84
  61.2 49.5 %while.15 = (s32[]{:T(128)}, f32[2,4,256]{2,1,0:T(4,128)S(1)}, f32[2,4,256]{2,1,0:T(4,128)S(1)}, f32[2,4,256,128]{3,2,1,0:T(8,128)}, s32[256]{0:T(256)S(1)}, /*i...) while((s32[]{:T(128)}, f32[2,4,256]{2,1,0:T(4,128)S(1)}, ...), condition=%wide.region_8.9_spmd.clone, body=%wide.region_5.8_spmd.clone.sunk | while | flops 551693056 | bytes 34223356 | solution.py:74
  63.9 2.7 fusion.33
  66.6 3.3 %fusion.34 = f32[2,4,256]{2,1,0:T(4,128)S(1)} fusion(f32[2,512,256,4]{2,1,3,0:T(8,128)} %get-tuple-element.232, f32[2,4,256]{2,1,0:T(4,128)S(1)} %select_maximum_fusion.2, pred[256,512]{0,1:T(8,128)(4,1)S(1)} %compare_and_fusion.3), kind=kLoop, calls=%fused_computation.6.clone.1 | loop fusion | flops 5240832 | bytes 4341760 | tf_op jit(solution)/shard_map/while/body/eval_jaxpr/reduce_sum | solution.py:64
  70.1 2.5 fusion.36
  75.4 2.7 fusion.33
  78.1 3.3 %fusion.34 = f32[2,4,256]{2,1,0:T(4,128)S(1)} fusion(f32[2,512,256,4]{2,1,3,0:T(8,128)} %get-tuple-element.232, f32[2,4,256]{2,1,0:T(4,128)S(1)} %select_maximum_fusion.2, pred[256,512]{0,1:T(8,128)(4,1)S(1)} %compare_and_fusion.3), kind=kLoop, calls=%fused_computation.6.clone.1 | loop fusion | flops 5240832 | bytes 4341760 | tf_op jit(solution)/shard_map/while/body/eval_jaxpr/reduce_sum | solution.py:64
  81.5 3.8 %fusion.36 = f32[2,4,256,128]{3,2,1,0:T(8,128)} fusion(f32[2,512,256,4]{2,1,3,0:T(8,128)S(1)} %copy-done, f32[2,4,256]{2,1,0:T(4,128)S(1)} %select_maximum_fusion.2, pred[256,512]{0,1:T(8,128)(4,1)S(1)} %compare_and_fusion.3, f32[2,4,256,128]{3,2,1,0:T(8,128)} %get-tuple-element.254, f32[2,4,256]{2,1,0:T(4,128)S(1)} %get-tuple-element.234, ...), kind=kOutput, calls=%fused_computation.9.clone.1 | convolution fusion | flops 274464768 | bytes 6701057 | tf_op jit(solution)/shard_map/while/body/eval_jaxpr/kgts,skd->kgtd/dot_general | solution.py:65
  88.0 2.7 fusion.33
  90.8 3.3 %fusion.34 = f32[2,4,256]{2,1,0:T(4,128)S(1)} fusion(f32[2,512,256,4]{2,1,3,0:T(8,128)} %get-tuple-element.232, f32[2,4,256]{2,1,0:T(4,128)S(1)} %select_maximum_fusion.2, pred[256,512]{0,1:T(8,128)(4,1)S(1)} %compare_and_fusion.3), kind=kLoop, calls=%fused_computation.6.clone.1 | loop fusion | flops 5240832 | bytes 4341760 | tf_op jit(solution)/shard_map/while/body/eval_jaxpr/reduce_sum | solution.py:64
  94.2 3.8 %fusion.36 = f32[2,4,256,128]{3,2,1,0:T(8,128)} fusion(f32[2,512,256,4]{2,1,3,0:T(8,128)S(1)} %copy-done, f32[2,4,256]{2,1,0:T(4,128)S(1)} %select_maximum_fusion.2, pred[256,512]{0,1:T(8,128)(4,1)S(1)} %compare_and_fusion.3, f32[2,4,256,128]{3,2,1,0:T(8,128)} %get-tuple-element.254, f32[2,4,256]{2,1,0:T(4,128)S(1)} %get-tuple-element.234, ...), kind=kOutput, calls=%fused_computation.9.clone.1 | convolution fusion | flops 274464768 | bytes 6701057 | tf_op jit(solution)/shard_map/while/body/eval_jaxpr/kgts,skd->kgtd/dot_general | solution.py:65
  100.7 2.7 fusion.33
  103.4 3.3 %fusion.34 = f32[2,4,256]{2,1,0:T(4,128)S(1)} fusion(f32[2,512,256,4]{2,1,3,0:T(8,128)} %get-tuple-element.232, f32[2,4,256]{2,1,0:T(4,128)S(1)} %select_maximum_fusion.2, pred[256,512]{0,1:T(8,128)(4,1)S(1)} %compare_and_fusion.3), kind=kLoop, calls=%fused_computation.6.clone.1 | loop fusion | flops 5240832 | bytes 4341760 | tf_op jit(solution)/shard_map/while/body/eval_jaxpr/reduce_sum | solution.py:64
  106.9 3.8 %fusion.36 = f32[2,4,256,128]{3,2,1,0:T(8,128)} fusion(f32[2,512,256,4]{2,1,3,0:T(8,128)S(1)} %copy-done, f32[2,4,256]{2,1,0:T(4,128)S(1)} %select_maximum_fusion.2, pred[256,512]{0,1:T(8,128)(4,1)S(1)} %compare_and_fusion.3, f32[2,4,256,128]{3,2,1,0:T(8,128)} %get-tuple-element.254, f32[2,4,256]{2,1,0:T(4,128)S(1)} %get-tuple-element.234, ...), kind=kOutput, calls=%fused_computation.9.clone.1 | convolution fusion | flops 274464768 | bytes 6701057 | tf_op jit(solution)/shard_map/while/body/eval_jaxpr/kgts,skd->kgtd/dot_general | solution.py:65
  110.7 1.6 copy.28
  112.3 12.1 %convolution_convert_fusion = bf16[256,8192]{1,0:T(8,128)(2,1)} fusion(bf16[256,1024]{0,1:T(8,128)(2,1)S(1)} %bitcast.75, bf16[1024,8192]{1,0:T(8,128)(2,1)} %param.15), kind=kOutput, calls=%fused_computation.26 | convolution fusion | flops 4297064448 | bytes 21495808 | tf_op jit(solution)/shard_map/dot_general | solution.py:80
  126.8 151.7 %all-reduce.2.cloned.1.call-done = bf16[256,8192]{1,0:T(8,128)(2,1)} async-done(((bf16[256,8192]{1,0:T(8,128)(2,1)}), bf16[256,8192]{1,0:T(8,128)(2,1)}) %all-reduce.2.cloned.1.call-update) | async-done | bytes 4194320 | tf_op jit(solution)/shard_map/psum | solution.py:92
  278.6 6.4 %convert_element_type.47 = f32[256,8192]{1,0:T(8,128)} convert(bf16[256,8192]{1,0:T(8,128)(2,1)} %all-reduce.2.cloned.1.call-done) | non-fusion elementwise | flops 2097152 | bytes 12582912 | tf_op jit(solution)/shard_map/convert_element_type | solution.py:92
  285.0 5.7 %gather_fusion = f32[64,8192]{1,0:T(8,128)S(1)} fusion(f32[256,8192]{1,0:T(8,128)} %convert_element_type.47, s32[1024]{0:T(1024)S(1)} %pad_clamp_fusion), kind=kCustom, calls=%fused_computation | custom fusion | bytes 4194560 | tf_op jit(solution)/shard_map/jit(_take)/gather | solution.py:96
  291.3 1.9 multiply_convert_fusion
  (79 shorter events, 14.1 us)
Async XLA Ops:
  7.2 27.2 %all-gather.3.cloned.1.call-start = ((), (), s32[]{:S(2)}) async-start(), calls=%async_computation | async-start | bytes 1179648 | tf_op jit(solution)/shard_map/all_gather | solution.py:39
  7.9 51.9 %all-gather.5.cloned.1.call-start = ((), (), s32[]{:S(2)}) async-start(), calls=%async_computation.1 | async-start | bytes 1179648 | tf_op jit(solution)/shard_map/all_gather | solution.py:40
  8.6 269.9 %all-reduce.2.cloned.1.call-start = ((), (), s32[]{:S(2)}) async-start(), calls=%async_computation.2 | async-start | bytes 8388608 | tf_op jit(solution)/shard_map/psum | solution.py:92
  66.6 3.4 %copy-start = (f32[2,512,256,4]{2,1,3,0:T(8,128)S(1)}, f32[2,512,256,4]{2,1,3,0:T(8,128)}, u32[]{:S(2)}) copy-start(f32[2,512,256,4]{2,1,3,0:T(8,128)} %get-tuple-element.232) | copy-start | bytes 12582916 | tf_op jit(solution)/shard_map/while
  78.1 3.4 %copy-start = (f32[2,512,256,4]{2,1,3,0:T(8,128)S(1)}, f32[2,512,256,4]{2,1,3,0:T(8,128)}, u32[]{:S(2)}) copy-start(f32[2,512,256,4]{2,1,3,0:T(8,128)} %get-tuple-element.232) | copy-start | bytes 12582916 | tf_op jit(solution)/shard_map/while
  90.8 3.4 %copy-start = (f32[2,512,256,4]{2,1,3,0:T(8,128)S(1)}, f32[2,512,256,4]{2,1,3,0:T(8,128)}, u32[]{:S(2)}) copy-start(f32[2,512,256,4]{2,1,3,0:T(8,128)} %get-tuple-element.232) | copy-start | bytes 12582916 | tf_op jit(solution)/shard_map/while
  103.4 3.4 %copy-start = (f32[2,512,256,4]{2,1,3,0:T(8,128)S(1)}, f32[2,512,256,4]{2,1,3,0:T(8,128)}, u32[]{:S(2)}) copy-start(f32[2,512,256,4]{2,1,3,0:T(8,128)} %get-tuple-element.232) | copy-start | bytes 12582916 | tf_op jit(solution)/shard_map/while
  124.4 0.7 copy-start.3
  285.0 5.7 %copy-start.1 = (bf16[64,8192]{1,0:T(8,128)(2,1)S(1)}, bf16[64,8192]{1,0:T(8,128)(2,1)}, u32[]{:S(2)}) copy-start(bf16[64,8192]{1,0:T(8,128)(2,1)} %param.16) | copy-start | bytes 3145732
  285.0 6.3 %copy-start.2 = (f32[8192]{0:T(1024)S(1)}, f32[8192]{0:T(1024)}, u32[]{:S(2)}) copy-start(f32[8192]{0:T(1024)} %param.17) | copy-start | bytes 98308
Sparse Core Ops, SparseCore 0:
  9.9 24.4 all-gather.2
  36.3 23.4 all-gather.4
  124.5 154.0 all-reduce.1
where the time goes:
time: 303 us; the launch traced here: 300 us
  waiting for transfers between devices  201 us (66%)
  matrix products  36.8 us (12%)
  other arithmetic  24.8 us (8%)
  local copies, waits for them, and re-layouts  20.6 us (7%)
  between operations  13.9 us (5%)
    psum x1, waiting for transfers between devices, on_device(): lax.psum(partial_rows.astype(jnp.float32).astype(jnp.bfloat16), 'tp')  152 us
    all_gather x1, waiting for transfers between devices, on_device(): value_piece = lax.all_gather(value_rows, 'ctx', axis=0, tiled=True)  24.1 us
    all_gather x1, waiting for transfers between devices, on_device(): key_piece = lax.all_gather(key_rows, 'ctx', axis=0, tiled=True)  23.4 us
    dot_general x4, matrix products, update(): jnp.einsum('kgts,skd->kgtd', exponent.astype(jnp.bfloat16), value_block,...  13.8 us
    reduce_sum x4, other arithmetic, update(): totals = totals * factor + jnp.sum(exponent, axis=-1)  13.4 us
    dot_general x1, matrix products, on_device(): jnp.dot(attended, out_proj, preferred_element_type=jnp.float32)  12.1 us
    dot_general x4, matrix products, update(): jnp.einsum('tkgd,skd->kgts', query_heads, key_block, preferred_element_ty...  10.9 us
    convert_element_type x1, other arithmetic, on_device(): lax.psum(partial_rows.astype(jnp.float32).astype(jnp.bfloat16), 'tp')  6.4 us
  transfers between devices with their start and end apart: 3, of which 3 were waited for; matrix products, arithmetic and copies ran while one was open for 2% of the time, Pallas kernels for 0%

commit v1 on v0

v1 whole, which is shorter than its diff:
```python
import functools
import math

import jax
import jax.numpy as jnp
from jax import lax
from jax.experimental import pallas as pl
from jax.experimental.pallas import tpu as pltpu
from jax.sharding import PartitionSpec as P

HEADS = 32
KV_HEADS = 8
HEAD_DIM = 128
GROUP = HEADS // KV_HEADS
TILE = 1024
CHUNK_BLOCKS = 5
MASKED = -1e30


def kernel(
    n_ctx,
    n_tp,
    q_ref,
    k_ref,
    v_ref,
    seg_ref,
    own_col_ref,
    own_row_ref,
    w_ref,
    res_ref,
    gain_ref,
    hid_ref,
    norm_ref,
    kbuf,
    vbuf,
    wbuf,
    attended,
    partial,
    landed,
    hidden,
    kv_send,
    kv_fwd,
    kv_recv,
    w_sem,
    row_send,
    row_recv,
):
    c = lax.axis_index("ctx")
    z = lax.axis_index("tp")
    rows = q_ref.shape[0]
    cap = res_ref.shape[0]
    tiles = wbuf.shape[0]
    window = n_ctx // 2
    kv_local = k_ref.shape[1] // HEAD_DIM
    scale = 1.0 / math.sqrt(HEAD_DIM)
    even = c % 2 == 0
    partner = c + 1 - 2 * (c % 2)
    strides = list(range(2, window + 1, 2))

    def weight_copy(t):
        cols = pl.ds(pl.multiple_of(t * TILE, TILE), TILE)
        return pltpu.make_async_copy(w_ref.at[:, cols], wbuf.at[t], w_sem.at[t])

    for t in range(tiles):
        weight_copy(t).start()

    barrier = pltpu.get_barrier_semaphore()

    def greet(cond, where):
        @pl.when(cond)
        def _():
            pl.semaphore_signal(barrier, inc=1, device_id=where)

        return cond.astype(jnp.int32)

    expected = 1
    pl.semaphore_signal(barrier, inc=1, device_id={"ctx": partner})
    for r in strides:
        expected = expected + greet(c + r < n_ctx, {"ctx": c + r})
        expected = expected + greet(c >= r, {"ctx": c - r})
    expected = expected + greet(z + 1 < n_tp, {"tp": z + 1})
    expected = expected + greet(z > 0, {"tp": z - 1})
    pl.semaphore_wait(barrier, expected)

    def kv_copies(src, place, send, where):
        dst = pl.ds(place * rows, rows)
        out = []
        for i, (own, buf) in enumerate(((k_ref, kbuf), (v_ref, vbuf))):
            ref = own if src is None else buf.at[pl.ds(src * rows, rows)]
            out.append(
                pltpu.make_async_remote_copy(
                    src_ref=ref,
                    dst_ref=buf.at[dst],
                    send_sem=send.at[i],
                    recv_sem=kv_recv.at[place, i],
                    device_id=where,
                )
            )
        return out

    def own_copies(r):
        return kv_copies(None, window - r, kv_send.at[r], {"ctx": c + r})

    def mate_copies():
        return kv_copies(None, window - 1, kv_send.at[0], {"ctx": partner})

    def forward_copies(r, place):
        return kv_copies(window - r, place, kv_fwd.at[r], {"ctx": partner})

    def landed_copies(r):
        return kv_copies(None, window - r, kv_send.at[r], {"ctx": partner})

    for r in reversed(strides):

        @pl.when(c + r < n_ctx)
        def _():
            for cp in own_copies(r):
                cp.start()

    @pl.when(even)
    def _():
        for cp in mate_copies():
            cp.start()

    kbuf[window * rows :, :] = k_ref[...]
    vbuf[window * rows :, :] = v_ref[...]
    for r in range(1, window + 1):

        @pl.when(c < r)
        def _():
            kbuf[(window - r) * rows : (window - r + 1) * rows, :] = jnp.zeros(k_ref.shape, k_ref.dtype)
            vbuf[(window - r) * rows : (window - r + 1) * rows, :] = jnp.zeros(v_ref.shape, v_ref.dtype)

    earlier = lax.broadcasted_iota(jnp.int32, (rows, rows), 0) < lax.broadcasted_iota(
        jnp.int32, (rows, rows), 1
    )
    same = own_col_ref[...] == own_row_ref[...]
    rank_row = jnp.sum(jnp.where(earlier & same, 1, 0), axis=0, keepdims=True)
    slot_row = own_row_ref[...] * cap + rank_row
    token_row = lax.broadcasted_iota(jnp.int32, (1, rows), 1)
    seg_here = seg_ref[c]

    for r in reversed(strides):

        @pl.when(c >= r)
        def _():
            for cp in landed_copies(r):
                cp.wait_recv()

            if r < window:

                @pl.when(even)
                def _():
                    for cp in forward_copies(r, window - r - 1):
                        cp.start()

            @pl.when(jnp.logical_not(even))
            def _():
                for cp in forward_copies(r, window - r + 1):
                    cp.start()

    for r in range(1, window, 2):

        @pl.when(c >= r)
        def _():
            for cp in landed_copies(r):
                cp.wait_recv()

    block_count = window + 1
    bounds = [
        (lo, min(lo + CHUNK_BLOCKS, block_count)) for lo in range(0, block_count, CHUNK_BLOCKS)
    ]

    def attend(d):
        slots = lax.broadcasted_iota(jnp.int32, (cap, rows), 0) + d * cap
        chosen = slots == slot_row
        filled = jnp.sum(jnp.where(chosen, 1.0, 0.0), axis=1, keepdims=True)
        q_pos = jnp.sum(jnp.where(chosen, token_row, 0), axis=1, keepdims=True) + c * rows
        q_seg = jnp.sum(jnp.where(chosen, seg_here, 0), axis=1, keepdims=True)
        q_slot = jnp.dot(
            jnp.where(chosen, 1.0, 0.0).astype(jnp.bfloat16),
            q_ref[...],
            preferred_element_type=jnp.float32,
        ).astype(jnp.bfloat16)
        states = [None] * kv_local
        for lo, hi in bounds:
            width = (hi - lo) * rows
            k_seg = jnp.concatenate(
                [seg_ref[jnp.maximum(c - window + j, 0)] for j in range(lo, hi)], axis=1
            )
            k_pos = lax.broadcasted_iota(jnp.int32, (1, width), 1) + (c - window + lo) * rows
            allowed = (k_seg == q_seg) & (k_pos <= q_pos) & (k_pos >= 0)
            bias = jnp.where(allowed, 0.0, MASKED)
            for k in range(kv_local):
                head = k * HEAD_DIM
                q = jnp.concatenate(
                    [
                        q_slot[:, (k * GROUP + g) * HEAD_DIM : (k * GROUP + g + 1) * HEAD_DIM]
                        for g in range(GROUP)
                    ],
                    axis=0,
                )
                s = lax.dot_general(
                    q,
                    kbuf[lo * rows : hi * rows, head : head + HEAD_DIM],
                    (((1,), (1,)), ((), ())),
                    preferred_element_type=jnp.float32,
                )
                s = s.reshape(GROUP, cap, width) + bias[None]
                top = jnp.max(s, axis=-1, keepdims=True)
                if states[k] is not None:
                    top = jnp.maximum(top, states[k][0])
                p = jnp.exp((s - top) * scale)
                total = jnp.sum(p, axis=-1, keepdims=True)
                o = jnp.dot(
                    p.reshape(GROUP * cap, width).astype(jnp.bfloat16),
                    vbuf[lo * rows : hi * rows, head : head + HEAD_DIM],
                    preferred_element_type=jnp.float32,
                ).reshape(GROUP, cap, HEAD_DIM)
                if states[k] is not None:
                    fade = jnp.exp((states[k][0] - top) * scale)
                    total = total + states[k][1] * fade
                    o = o + states[k][2] * fade
                states[k] = (top, total, o)
        for k in range(kv_local):
            _, total, o = states[k]
            o = jnp.where(filled[None] > 0, o / total, 0.0).astype(jnp.bfloat16)
            for g in range(GROUP):
                col = (k * GROUP + g) * HEAD_DIM
                attended[d, :, col : col + HEAD_DIM] = o[g]

    def right_copy(d, t):
        return pltpu.make_async_remote_copy(
            src_ref=partial.at[d, t],
            dst_ref=landed.at[d + 1, t],
            send_sem=row_send.at[d, t],
            recv_sem=row_recv.at[d + 1, t],
            device_id={"tp": z + 1},
        )

    def left_copy(d, t):
        return pltpu.make_async_remote_copy(
            src_ref=partial.at[d, t],
            dst_ref=landed.at[d, t],
            send_sem=row_send.at[d, t],
            recv_sem=row_recv.at[d, t],
            device_id={"tp": z - 1},
        )

    def each_tile(body):
        def step(t, carry):
            body(t)
            return carry

        lax.fori_loop(0, tiles, step, 0)

    low = z < (n_tp // 2)
    first = jnp.where(low, n_tp - 1, 0)
    rest = jnp.where(low, 0, 1)
    attend(first)

    def project_first(t):
        weight_copy(t).wait()
        partial[first, t] = jnp.dot(
            attended[first], wbuf[t], preferred_element_type=jnp.float32
        ).astype(jnp.bfloat16)

        @pl.when(z == 0)
        def _():
            right_copy(n_tp - 1, t).start()

        @pl.when(z == n_tp - 1)
        def _():
            left_copy(0, t).start()

    each_tile(project_first)

    def attend_rest(i, carry):
        attend(rest + i)
        return carry

    lax.fori_loop(0, n_tp - 1, attend_rest, 0)

    def project_rest(t):
        a = attended[pl.ds(rest, n_tp - 1)].reshape((n_tp - 1) * cap, attended.shape[2])
        y = jnp.dot(a, wbuf[t], preferred_element_type=jnp.float32).astype(jnp.bfloat16)
        for i in range(n_tp - 1):
            partial[rest + i, t] = y[i * cap : (i + 1) * cap]

        @pl.when(z == 0)
        def _():
            right_copy(n_tp - 2, t).start()

        @pl.when(z == n_tp - 1)
        def _():
            left_copy(1, t).start()

    each_tile(project_rest)

    for j in range(2, n_tp - 1):

        def send_more(t):
            @pl.when(z == 0)
            def _():
                right_copy(n_tp - 1 - j, t).start()

            @pl.when(z == n_tp - 1)
            def _():
                left_copy(j, t).start()

        each_tile(send_more)

    for j in range(n_tp - 1):

        def pump(t):
            d_right = n_tp - 1 - j
            d_left = j

            @pl.when((z > 0) & (z < d_right))
            def _():
                cp = right_copy(d_right, t)
                cp.wait_recv()
                partial[d_right, t] = (
                    partial[d_right, t].astype(jnp.float32)
                    + landed[d_right + 1, t].astype(jnp.float32)
                ).astype(jnp.bfloat16)
                cp.start()

            @pl.when((z < n_tp - 1) & (z > d_left))
            def _():
                cp = left_copy(d_left, t)
                cp.wait_recv()
                partial[d_left, t] = (
                    partial[d_left, t].astype(jnp.float32)
                    + landed[d_left, t].astype(jnp.float32)
                ).astype(jnp.bfloat16)
                cp.start()

        each_tile(pump)

    def finish(t, squares):
        cols = pl.ds(pl.multiple_of(t * TILE, TILE), TILE)
        hidden[t] = res_ref[:, cols].astype(jnp.float32) + partial[z, t].astype(jnp.float32)

        @pl.when(z > 0)
        def _():
            right_copy(z, t).wait_recv()
            hidden[t] = hidden[t] + landed[z + 1, t].astype(jnp.float32)

        @pl.when(z < n_tp - 1)
        def _():
            left_copy(z, t).wait_recv()
            hidden[t] = hidden[t] + landed[z, t].astype(jnp.float32)

        h = hidden[t]
        hid_ref[:, cols] = h.astype(hid_ref.dtype)
        return squares + jnp.sum(h * h, axis=-1, keepdims=True)

    squares = lax.fori_loop(0, tiles, finish, jnp.zeros((cap, 1), jnp.float32))
    inverse = lax.rsqrt(squares / (tiles * TILE) + 1e-05)

    def scale_tile(t):
        cols = pl.ds(pl.multiple_of(t * TILE, TILE), TILE)
        norm_ref[:, cols] = (hidden[t] * inverse * gain_ref[:, cols]).astype(norm_ref.dtype)

    each_tile(scale_tile)

    for r in strides:

        @pl.when(c + r < n_ctx)
        def _():
            for cp in own_copies(r):
                cp.wait_send()

        @pl.when(c >= r)
        def _():
            if r < window:

                @pl.when(even)
                def _():
                    for cp in forward_copies(r, window - r - 1):
                        cp.wait_send()

            @pl.when(jnp.logical_not(even))
            def _():
                for cp in forward_copies(r, window - r + 1):
                    cp.wait_send()

    @pl.when(even)
    def _():
        for cp in mate_copies():
            cp.wait_send()

    for d in range(n_tp):

        def sent(t):
            @pl.when(z < d)
            def _():
                right_copy(d, t).wait_send()

            @pl.when(z > d)
            def _():
                left_copy(d, t).wait_send()

        each_tile(sent)


def on_device(n_ctx, n_tp, queries, key_rows, value_rows, segments, owner_ids, out_proj, residual, norm_gain):
    rows, width = queries.shape
    cap, model = residual.shape
    tiles = model // TILE
    keys = (n_ctx // 2 + 1) * rows
    vmem = pl.BlockSpec(memory_space=pltpu.VMEM)
    out = jax.ShapeDtypeStruct((cap, model), jnp.bfloat16)
    return pl.pallas_call(
        functools.partial(kernel, n_ctx, n_tp),
        out_shape=(out, out),
        in_specs=[vmem] * 6 + [pl.BlockSpec(memory_space=pl.ANY)] + [vmem] * 2,
        out_specs=(vmem, vmem),
        scratch_shapes=[
            pltpu.VMEM((keys, key_rows.shape[1]), jnp.bfloat16),
            pltpu.VMEM((keys, key_rows.shape[1]), jnp.bfloat16),
            pltpu.VMEM((tiles, width, TILE), jnp.bfloat16),
            pltpu.VMEM((n_tp, cap, width), jnp.bfloat16),
            pltpu.VMEM((n_tp, tiles, cap, TILE), jnp.bfloat16),
            pltpu.VMEM((n_tp + 1, tiles, cap, TILE), jnp.bfloat16),
            pltpu.VMEM((tiles, cap, TILE), jnp.float32),
            pltpu.SemaphoreType.DMA((n_ctx // 2 + 1, 2)),
            pltpu.SemaphoreType.DMA((n_ctx // 2 + 1, 2)),
            pltpu.SemaphoreType.DMA((n_ctx // 2 + 1, 2)),
            pltpu.SemaphoreType.DMA((tiles,)),
            pltpu.SemaphoreType.DMA((n_tp, tiles)),
            pltpu.SemaphoreType.DMA((n_tp + 1, tiles)),
        ],
        compiler_params=pltpu.CompilerParams(
            collective_id=0, has_side_effects=True, vmem_limit_bytes=60 * 1024 * 1024
        ),
    )(
        queries,
        key_rows,
        value_rows,
        segments.reshape(n_ctx, 1, rows),
        owner_ids,
        owner_ids.reshape(1, rows),
        out_proj,
        residual,
        norm_gain.reshape(1, model),
    )


def solution(mesh):
    placed = (
        P("ctx", "tp"),
        P("ctx", "tp"),
        P("ctx", "tp"),
        P(),
        P("ctx", None),
        P("tp", None),
        P(("ctx", "tp"), None),
        P(),
    )
    return jax.shard_map(
        functools.partial(on_device, mesh.shape["ctx"], mesh.shape["tp"]),
        mesh=mesh,
        in_specs=placed,
        out_specs=(P(("ctx", "tp"), None), P(("ctx", "tp"), None)),
        check_vma=False,
    )
```

time: 303 us -> 128 us (0.42)
  waiting for transfers between devices: 201 us -> 0 us
  Pallas kernels: 0 us -> 121 us
  matrix products: 36.8 us -> 0 us
  other arithmetic: 24.8 us -> 0 us
  local copies, waits for them, and re-layouts: 20.6 us -> 6 us
  between operations: 13.9 us -> 0.64 us
    psum x1 -> x0, waiting for transfers between devices: 152 us -> none  [on_device(): lax.psum(partial_rows.astype(jnp.float32).astype(jnp.bfloat16), 'tp')]
    pallas_call x0 -> x1, Pallas kernels: none -> 121 us  [on_device(): pl.pallas_call(functools.partial(kernel, n_ctx, n_tp), out_shape=(out, ou...]
    all_gather x2 -> x0, waiting for transfers between devices: 47.4 us -> none  [the longest x1 24.1 us: on_device(): value_piece = lax.all_gather(value_rows, 'ctx', axis=0, tiled=True)]
    dot_general x9 -> x0, matrix products: 36.8 us -> none  [the longest x4 13.8 us: update(): jnp.einsum('kgts,skd->kgtd', exponent.astype(jnp.bfloat16), value_block,...]
    reduce_sum x7 -> x0, other arithmetic: 14.1 us -> none  [the longest x4 13.4 us: update(): totals = totals * factor + jnp.sum(exponent, axis=-1)]
    convert_element_type x4 -> x0, other arithmetic: 8.4 us -> none  [the longest x1 6.4 us: on_device(): lax.psum(partial_rows.astype(jnp.float32).astype(jnp.bfloat16), 'tp')]
    dynamic_slice x13 -> x0, local copies, waits for them, and re-layouts: 7.95 us -> none  [the longest x8 4.13 us: on_device(): lax.scan(update, carried, (jnp.arange(block_count, dtype=jnp.int32), key_...]
    gather x1 -> x0, local copies, waits for them, and re-layouts: 5.65 us -> none  [on_device(): jnp.take(summed, token_index, axis=0)]
  transfers between devices with their start and end apart: 3 -> 0, of which waited for: 3 -> 0; matrix products, arithmetic and copies ran while one was open for 2% -> 0% of each run, Pallas kernels for 0% -> 0%
where the time goes in v1:
time: 128 us
  Pallas kernels  121 us (95%)
  local copies, waits for them, and re-layouts  6 us (5%)
    pallas_call x1, Pallas kernels, on_device(): pl.pallas_call(functools.partial(kernel, n_ctx, n_tp), out_shape=(out, ou...  121 us
    unnamed x3, local copies, waits for them, and re-layouts  6 us

profile of v1, /device:TPU:20, one launch (start us, length us, event | category | flops | bytes accessed | tf_op | source)
XLA Modules:
  0.0 127.7 jit_solution(1600496757071554540)
XLA Ops:
  0.6 1.5 %copy.10.own_col_ref = s32[256,1]{1,0:T(8,128)} copy(s32[256,1]{0,1:T(1,128)} %param.12) | data formatting | bytes 2048 | tf_op args[4]
  2.1 121.0 %shard_map.95 = (bf16[64,8192]{1,0:T(8,128)(2,1)}, bf16[64,8192]{1,0:T(8,128)(2,1)}) custom-call(bf16[256,1024]{1,0:T(8,128)(2,1)} %q_ref.1, bf16[256,256]{1,0:T(8,128)(2,1)} %k_ref.1, bf16[256,256]{1,0:T(8,128)(2,1)} %v_ref.1, s32[8,1,256]{2,1,0:T(1,128)} %bitcast.4, s32[256,1]{1,0:T(8,128)} %copy.10.own_col_ref, s32[1,256]{1,0:T(1,128)} %bitcast.5, ...), custom_call_target="tpu_custom_call" | custom-call | tf_op jit(solution)/shard_map/pallas_call | solution.py:415
  123.1 2.3 %copy.13 = bf16[64,8192]{1,0:T(8,128)(2,1)} copy(bf16[64,8192]{1,0:T(8,128)(2,1)} %get-tuple-element.4) | data formatting | bytes 2097152
  125.4 2.3 %copy.14 = bf16[64,8192]{1,0:T(8,128)(2,1)} copy(bf16[64,8192]{1,0:T(8,128)(2,1)} %get-tuple-element.5) | data formatting | bytes 2097152

commit v2 on v1

--- a/solution.py
+++ b/solution.py
@@ -24,20 +24,17 @@
     k_ref,
     v_ref,
     seg_ref,
-    own_col_ref,
     own_row_ref,
     w_ref,
     res_ref,
-    gain_ref,
     hid_ref,
-    norm_ref,
+    inv_ref,
     kbuf,
     vbuf,
     wbuf,
     attended,
     partial,
     landed,
-    hidden,
     kv_send,
     kv_fwd,
     kv_recv,
@@ -131,11 +128,11 @@
             kbuf[(window - r) * rows : (window - r + 1) * rows, :] = jnp.zeros(k_ref.shape, k_ref.dtype)
             vbuf[(window - r) * rows : (window - r + 1) * rows, :] = jnp.zeros(v_ref.shape, v_ref.dtype)
 
-    earlier = lax.broadcasted_iota(jnp.int32, (rows, rows), 0) < lax.broadcasted_iota(
-        jnp.int32, (rows, rows), 1
-    )
-    same = own_col_ref[...] == own_row_ref[...]
-    rank_row = jnp.sum(jnp.where(earlier & same, 1, 0), axis=0, keepdims=True)
+    down = lax.broadcasted_iota(jnp.int32, (rows, rows), 0)
+    along = lax.broadcasted_iota(jnp.int32, (rows, rows), 1)
+    own_col = jnp.sum(jnp.where(down == along, own_row_ref[...], 0), axis=1, keepdims=True)
+    same = own_col == own_row_ref[...]
+    rank_row = jnp.sum(jnp.where((down < along) & same, 1, 0), axis=0, keepdims=True)
     slot_row = own_row_ref[...] * cap + rank_row
     token_row = lax.broadcasted_iota(jnp.int32, (1, rows), 1)
     seg_here = seg_ref[c]
@@ -340,30 +337,23 @@
 
     def finish(t, squares):
         cols = pl.ds(pl.multiple_of(t * TILE, TILE), TILE)
-        hidden[t] = res_ref[:, cols].astype(jnp.float32) + partial[z, t].astype(jnp.float32)
+        hid_ref[:, cols] = res_ref[:, cols].astype(jnp.float32) + partial[z, t].astype(jnp.float32)
 
         @pl.when(z > 0)
         def _():
             right_copy(z, t).wait_recv()
-            hidden[t] = hidden[t] + landed[z + 1, t].astype(jnp.float32)
+            hid_ref[:, cols] = hid_ref[:, cols] + landed[z + 1, t].astype(jnp.float32)
 
         @pl.when(z < n_tp - 1)
         def _():
             left_copy(z, t).wait_recv()
-            hidden[t] = hidden[t] + landed[z, t].astype(jnp.float32)
-
-        h = hidden[t]
-        hid_ref[:, cols] = h.astype(hid_ref.dtype)
+            hid_ref[:, cols] = hid_ref[:, cols] + landed[z, t].astype(jnp.float32)
+
+        h = hid_ref[:, cols]
         return squares + jnp.sum(h * h, axis=-1, keepdims=True)
 
     squares = lax.fori_loop(0, tiles, finish, jnp.zeros((cap, 1), jnp.float32))
-    inverse = lax.rsqrt(squares / (tiles * TILE) + 1e-05)
-
-    def scale_tile(t):
-        cols = pl.ds(pl.multiple_of(t * TILE, TILE), TILE)
-        norm_ref[:, cols] = (hidden[t] * inverse * gain_ref[:, cols]).astype(norm_ref.dtype)
-
-    each_tile(scale_tile)
+    inv_ref[...] = jnp.broadcast_to(lax.rsqrt(squares / (tiles * TILE) + 1e-05), inv_ref.shape)
 
     for r in strides:
 
@@ -411,11 +401,13 @@
     tiles = model // TILE
     keys = (n_ctx // 2 + 1) * rows
     vmem = pl.BlockSpec(memory_space=pltpu.VMEM)
-    out = jax.ShapeDtypeStruct((cap, model), jnp.bfloat16)
-    return pl.pallas_call(
+    hidden, inverse = pl.pallas_call(
         functools.partial(kernel, n_ctx, n_tp),
-        out_shape=(out, out),
-        in_specs=[vmem] * 6 + [pl.BlockSpec(memory_space=pl.ANY)] + [vmem] * 2,
+        out_shape=(
+            jax.ShapeDtypeStruct((cap, model), jnp.float32),
+            jax.ShapeDtypeStruct((cap, HEAD_DIM), jnp.float32),
+        ),
+        in_specs=[vmem] * 5 + [pl.BlockSpec(memory_space=pl.ANY), vmem],
         out_specs=(vmem, vmem),
         scratch_shapes=[
             pltpu.VMEM((keys, key_rows.shape[1]), jnp.bfloat16),
@@ -424,7 +416,6 @@
             pltpu.VMEM((n_tp, cap, width), jnp.bfloat16),
             pltpu.VMEM((n_tp, tiles, cap, TILE), jnp.bfloat16),
             pltpu.VMEM((n_tp + 1, tiles, cap, TILE), jnp.bfloat16),
-            pltpu.VMEM((tiles, cap, TILE), jnp.float32),
             pltpu.SemaphoreType.DMA((n_ctx // 2 + 1, 2)),
             pltpu.SemaphoreType.DMA((n_ctx // 2 + 1, 2)),
             pltpu.SemaphoreType.DMA((n_ctx // 2 + 1, 2)),
@@ -440,12 +431,12 @@
         key_rows,
         value_rows,
         segments.reshape(n_ctx, 1, rows),
-        owner_ids,
         owner_ids.reshape(1, rows),
         out_proj,
         residual,
-        norm_gain.reshape(1, model),
     )
+    normed = hidden * inverse[:, :1] * norm_gain
+    return (hidden.astype(jnp.bfloat16), normed.astype(jnp.bfloat16))
 
 
 def solution(mesh):

time: 128 us -> 126 us (0.984)
  local copies, waits for them, and re-layouts: 6 us -> 0.87 us
  other arithmetic: 0 us -> 3.87 us
    unnamed x3 -> x2, local copies, waits for them, and re-layouts: 6 us -> 0.01 us
    convert_element_type x0 -> x1, other arithmetic: none -> 3.87 us  [on_device(): return (hidden.astype(jnp.bfloat16), normed.astype(jnp.bfloat16))]
where the time goes in v2:
time: 126 us
  Pallas kernels  121 us (96%)
  other arithmetic  3.87 us (3%)
    pallas_call x1, Pallas kernels, on_device(): pl.pallas_call(functools.partial(kernel, n_ctx, n_tp), out_shape=(jax.Sha...  121 us
    convert_element_type x1, other arithmetic, on_device(): return (hidden.astype(jnp.bfloat16), normed.astype(jnp.bfloat16))  3.87 us

profile of v2, /device:TPU:20, one launch (start us, length us, event | category | flops | bytes accessed | tf_op | source)
XLA Modules:
  0.0 126.2 jit_solution(5489587036119012041)
XLA Ops:
  0.6 0.0 copy-start
  0.6 120.8 %shard_map.95 = (f32[64,8192]{1,0:T(8,128)}, f32[64,128]{1,0:T(8,128)}) custom-call(bf16[256,1024]{1,0:T(8,128)(2,1)} %q_ref.1, bf16[256,256]{1,0:T(8,128)(2,1)} %k_ref.1, bf16[256,256]{1,0:T(8,128)(2,1)} %v_ref.1, s32[8,1,256]{2,1,0:T(1,128)} %bitcast.2, s32[1,256]{1,0:T(1,128)} %bitcast.3, bf16[1024,8192]{1,0:T(8,128)(2,1)} %w_ref.1, bf16[64,8192]{1,0:T(8,128)(2,1)} %res_ref.1), custom_call_target="tpu_custom_call" | custom-call | tf_op jit(solution)/shard_map/pallas_call | solution.py:404
  121.5 0.9 slice_reduce_fusion
  122.3 0.0 copy-done
  122.3 3.9 %multiply_convert_fusion = (bf16[64,8192]{1,0:T(8,128)(2,1)}, bf16[64,8192]{1,0:T(8,128)(2,1)}) fusion(f32[64,8192]{1,0:T(8,128)} %get-tuple-element.4, f32[8192]{0:T(1024)S(1)} %copy-done, f32[64]{0:T(128)S(1)} %slice_reduce_fusion), kind=kLoop, calls=%fused_computation | loop fusion | flops 2097152 | bytes 4227328 | tf_op jit(solution)/shard_map/convert_element_type | solution.py:439
Async XLA Ops:
  0.6 121.7 %copy-start = (f32[8192]{0:T(1024)S(1)}, f32[8192]{0:T(1024)}, u32[]{:S(2)}) copy-start(f32[8192]{0:T(1024)} %param.15) | copy-start | bytes 98308

commit v3 on v2

--- a/solution.py
+++ b/solution.py
@@ -14,6 +14,7 @@
 GROUP = HEADS // KV_HEADS
 TILE = 1024
 CHUNK_BLOCKS = 5
+FAR_TILES = 2
 MASKED = -1e30
 
 
@@ -35,12 +36,19 @@
     attended,
     partial,
     landed,
+    wfar,
+    attfar,
     kv_send,
     kv_fwd,
     kv_recv,
     w_sem,
     row_send,
     row_recv,
+    ship_send,
+    spread_send,
+    spread_recv,
+    far_send,
+    far_recv,
 ):
     c = lax.axis_index("ctx")
     z = lax.axis_index("tp")
@@ -72,12 +80,63 @@
 
     expected = 1
     pl.semaphore_signal(barrier, inc=1, device_id={"ctx": partner})
-    for r in strides:
-        expected = expected + greet(c + r < n_ctx, {"ctx": c + r})
-        expected = expected + greet(c >= r, {"ctx": c - r})
+    for r in range(2, n_ctx, 2):
+        pl.semaphore_signal(barrier, inc=1, device_id={"ctx": (c + r) % n_ctx})
+        expected = expected + 1
     expected = expected + greet(z + 1 < n_tp, {"tp": z + 1})
     expected = expected + greet(z > 0, {"tp": z - 1})
     pl.semaphore_wait(barrier, expected)
+
+    near = tiles - FAR_TILES
+    at_end = (z == 0) | (z == n_tp - 1)
+    helper = (z == 1) | (z == n_tp - 2)
+    inward = jnp.where(z == 0, 1, n_tp - 2)
+    share = w_ref.shape[0] // n_ctx
+
+    def w_rows(who):
+        return pl.ds(pl.multiple_of(who * share, share), share)
+
+    def ship_copy(f):
+        return pltpu.make_async_remote_copy(
+            src_ref=w_ref.at[w_rows(c), pl.ds((near + f) * TILE, TILE)],
+            dst_ref=wfar.at[f, w_rows(c)],
+            send_sem=ship_send.at[f],
+            recv_sem=spread_recv.at[0, f],
+            device_id={"tp": inward},
+        )
+
+    def spread_copy(r, f):
+        return pltpu.make_async_remote_copy(
+            src_ref=wfar.at[f, w_rows(c)],
+            dst_ref=wfar.at[f, w_rows(c)],
+            send_sem=spread_send.at[r, f],
+            recv_sem=spread_recv.at[r, f],
+            device_id={"ctx": (c + r) % n_ctx},
+        )
+
+    def mate_weights(r, f):
+        slice_rows = w_rows((c - r + n_ctx) % n_ctx)
+        return pltpu.make_async_remote_copy(
+            src_ref=wfar.at[f, slice_rows],
+            dst_ref=wfar.at[f, slice_rows],
+            send_sem=spread_send.at[r + 1, f],
+            recv_sem=spread_recv.at[(r + 2 - 2 * (c % 2) - 1 + n_ctx) % n_ctx, f],
+            device_id={"ctx": partner},
+        )
+
+    def far_copy(d):
+        return pltpu.make_async_remote_copy(
+            src_ref=attended.at[d],
+            dst_ref=attfar.at[d],
+            send_sem=far_send.at[d],
+            recv_sem=far_recv.at[d],
+            device_id={"tp": inward},
+        )
+
+    @pl.when(at_end)
+    def _():
+        for f in range(FAR_TILES):
+            ship_copy(f).start()
 
     def kv_copies(src, place, send, where):
         dst = pl.ds(place * rows, rows)
@@ -244,16 +303,25 @@
             device_id={"tp": z - 1},
         )
 
-    def each_tile(body):
+    def each_tile(body, start=0, stop=tiles):
         def step(t, carry):
             body(t)
             return carry
 
-        lax.fori_loop(0, tiles, step, 0)
+        lax.fori_loop(start, stop, step, 0)
 
     low = z < (n_tp // 2)
     first = jnp.where(low, n_tp - 1, 0)
     rest = jnp.where(low, 0, 1)
+
+    @pl.when(helper)
+    def _():
+        for f in range(FAR_TILES):
+            spread_copy(0, f).wait_recv()
+            for r in range(2, n_ctx, 2):
+                spread_copy(r, f).start()
+            mate_weights(0, f).start()
+
     attend(first)
 
     def project_first(t):
@@ -262,11 +330,11 @@
             attended[first], wbuf[t], preferred_element_type=jnp.float32
         ).astype(jnp.bfloat16)
 
-        @pl.when(z == 0)
+        @pl.when((z == 0) & (t < near))
         def _():
             right_copy(n_tp - 1, t).start()
 
-        @pl.when(z == n_tp - 1)
+        @pl.when((z == n_tp - 1) & (t < near))
         def _():
             left_copy(0, t).start()
 
@@ -277,6 +345,11 @@
         return carry
 
     lax.fori_loop(0, n_tp - 1, attend_rest, 0)
+
+    @pl.when(at_end)
+    def _():
+        for i in range(n_tp - 1):
+            far_copy(jnp.where(z == 0, n_tp - 1 - i, i)).start()
 
     def project_rest(t):
         a = attended[pl.ds(rest, n_tp - 1)].reshape((n_tp - 1) * cap, attended.shape[2])
@@ -284,11 +357,11 @@
         for i in range(n_tp - 1):
             partial[rest + i, t] = y[i * cap : (i + 1) * cap]
 
-        @pl.when(z == 0)
+        @pl.when((z == 0) & (t < near))
         def _():
             right_copy(n_tp - 2, t).start()
 
-        @pl.when(z == n_tp - 1)
+        @pl.when((z == n_tp - 1) & (t < near))
         def _():
             left_copy(1, t).start()
 
@@ -305,46 +378,89 @@
             def _():
                 left_copy(j, t).start()
 
-        each_tile(send_more)
-
+        each_tile(send_more, 0, near)
+
+    def pump(j, t):
+        d_right = n_tp - 1 - j
+        d_left = j
+
+        @pl.when((z > 0) & (z < d_right) & ((t < near) | (z > 1)))
+        def _():
+            cp = right_copy(d_right, t)
+            cp.wait_recv()
+            partial[d_right, t] = (
+                partial[d_right, t].astype(jnp.float32)
+                + landed[d_right + 1, t].astype(jnp.float32)
+            ).astype(jnp.bfloat16)
+            cp.start()
+
+        @pl.when((z < n_tp - 1) & (z > d_left) & ((t < near) | (z < n_tp - 2)))
+        def _():
+            cp = left_copy(d_left, t)
+            cp.wait_recv()
+            partial[d_left, t] = (
+                partial[d_left, t].astype(jnp.float32)
+                + landed[d_left, t].astype(jnp.float32)
+            ).astype(jnp.bfloat16)
+            cp.start()
+
+    @pl.when(helper)
+    def _():
+        for f in range(FAR_TILES):
+            for r in range(2, n_ctx, 2):
+                spread_copy(r, f).wait_recv()
+                mate_weights(r, f).start()
+
+    each_tile(functools.partial(pump, 0), 0, near)
+
+    @pl.when(helper)
+    def _():
+        base = jnp.where(z == 1, 1, 0)
+        for f in range(FAR_TILES):
+            for r in range(1, n_ctx, 2):
+                spread_copy(r, f).wait_recv()
+        for i in range(n_tp - 1):
+            far_copy(base + i).wait_recv()
+
+        def far_tile(t):
+            a = attfar[pl.ds(base, n_tp - 1)].reshape((n_tp - 1) * cap, attended.shape[2])
+            y = jnp.dot(a, wfar[t - near], preferred_element_type=jnp.float32)
+            for i in range(n_tp - 1):
+                d = base + i
+                partial[d, t] = (
+                    partial[d, t].astype(jnp.float32) + y[i * cap : (i + 1) * cap]
+                ).astype(jnp.bfloat16)
+
+        each_tile(far_tile, near, tiles)
+
+        for j in range(n_tp - 2):
+
+            def far_send_on(t):
+                @pl.when(z == 1)
+                def _():
+                    right_copy(n_tp - 1 - j, t).start()
+
+                @pl.when(z == n_tp - 2)
+                def _():
+                    left_copy(j, t).start()
+
+            each_tile(far_send_on, near, tiles)
+
+    for j in range(1, n_tp - 1):
+        each_tile(functools.partial(pump, j), 0, near)
     for j in range(n_tp - 1):
-
-        def pump(t):
-            d_right = n_tp - 1 - j
-            d_left = j
-
-            @pl.when((z > 0) & (z < d_right))
-            def _():
-                cp = right_copy(d_right, t)
-                cp.wait_recv()
-                partial[d_right, t] = (
-                    partial[d_right, t].astype(jnp.float32)
-                    + landed[d_right + 1, t].astype(jnp.float32)
-                ).astype(jnp.bfloat16)
-                cp.start()
-
-            @pl.when((z < n_tp - 1) & (z > d_left))
-            def _():
-                cp = left_copy(d_left, t)
-                cp.wait_recv()
-                partial[d_left, t] = (
-                    partial[d_left, t].astype(jnp.float32)
-                    + landed[d_left, t].astype(jnp.float32)
-                ).astype(jnp.bfloat16)
-                cp.start()
-
-        each_tile(pump)
+        each_tile(functools.partial(pump, j), near, tiles)
 
     def finish(t, squares):
         cols = pl.ds(pl.multiple_of(t * TILE, TILE), TILE)
         hid_ref[:, cols] = res_ref[:, cols].astype(jnp.float32) + partial[z, t].astype(jnp.float32)
 
-        @pl.when(z > 0)
+        @pl.when((z > 0) & ((t < near) | (z > 1)))
         def _():
             right_copy(z, t).wait_recv()
             hid_ref[:, cols] = hid_ref[:, cols] + landed[z + 1, t].astype(jnp.float32)
 
-        @pl.when(z < n_tp - 1)
+        @pl.when((z < n_tp - 1) & ((t < near) | (z < n_tp - 2)))
         def _():
             left_copy(z, t).wait_recv()
             hid_ref[:, cols] = hid_ref[:, cols] + landed[z, t].astype(jnp.float32)
@@ -384,15 +500,36 @@
     for d in range(n_tp):
 
         def sent(t):
-            @pl.when(z < d)
+            @pl.when((z < d) & ((t < near) | (z > 0)))
             def _():
                 right_copy(d, t).wait_send()
 
-            @pl.when(z > d)
+            @pl.when((z > d) & ((t < near) | (z < n_tp - 1)))
             def _():
                 left_copy(d, t).wait_send()
 
         each_tile(sent)
+
+    @pl.when(at_end)
+    def _():
+        for f in range(FAR_TILES):
+            ship_copy(f).wait_send()
+        for i in range(n_tp - 1):
+            far_copy(jnp.where(z == 0, n_tp - 1 - i, i)).wait_send()
+
+    @pl.when(helper)
+    def _():
+        for f in range(FAR_TILES):
+            mate_weights(0, f).wait_send()
+            for r in range(2, n_ctx, 2):
+                spread_copy(r, f).wait_send()
+                mate_weights(r, f).wait_send()
+
+
+def scale_rows(hidden_ref, inverse_ref, gain_ref, hid_ref, norm_ref):
+    h = hidden_ref[...]
+    hid_ref[...] = h.astype(hid_ref.dtype)
+    norm_ref[...] = (h * inverse_ref[:, :1] * gain_ref[...]).astype(norm_ref.dtype)
 
 
 def on_device(n_ctx, n_tp, queries, key_rows, value_rows, segments, owner_ids, out_proj, residual, norm_gain):
@@ -416,12 +553,19 @@
             pltpu.VMEM((n_tp, cap, width), jnp.bfloat16),
             pltpu.VMEM((n_tp, tiles, cap, TILE), jnp.bfloat16),
             pltpu.VMEM((n_tp + 1, tiles, cap, TILE), jnp.bfloat16),
+            pltpu.VMEM((FAR_TILES, width, TILE), jnp.bfloat16),
+            pltpu.VMEM((n_tp, cap, width), jnp.bfloat16),
             pltpu.SemaphoreType.DMA((n_ctx // 2 + 1, 2)),
             pltpu.SemaphoreType.DMA((n_ctx // 2 + 1, 2)),
             pltpu.SemaphoreType.DMA((n_ctx // 2 + 1, 2)),
             pltpu.SemaphoreType.DMA((tiles,)),
             pltpu.SemaphoreType.DMA((n_tp, tiles)),
             pltpu.SemaphoreType.DMA((n_tp + 1, tiles)),
+            pltpu.SemaphoreType.DMA((FAR_TILES,)),
+            pltpu.SemaphoreType.DMA((n_ctx, FAR_TILES)),
+            pltpu.SemaphoreType.DMA((n_ctx, FAR_TILES)),
+            pltpu.SemaphoreType.DMA((n_tp,)),
+            pltpu.SemaphoreType.DMA((n_tp,)),
         ],
         compiler_params=pltpu.CompilerParams(
             collective_id=0, has_side_effects=True, vmem_limit_bytes=60 * 1024 * 1024
@@ -435,8 +579,19 @@
         out_proj,
         residual,
     )
-    normed = hidden * inverse[:, :1] * norm_gain
-    return (hidden.astype(jnp.bfloat16), normed.astype(jnp.bfloat16))
+    out = jax.ShapeDtypeStruct((cap, model), jnp.bfloat16)
+    part = pl.BlockSpec((16, model), lambda i: (i, 0))
+    return pl.pallas_call(
+        scale_rows,
+        grid=(cap // 16,),
+        out_shape=(out, out),
+        in_specs=[
+            part,
+            pl.BlockSpec((16, HEAD_DIM), lambda i: (i, 0)),
+            pl.BlockSpec((1, model), lambda i: (0, 0)),
+        ],
+        out_specs=(part, part),
+    )(hidden, inverse, norm_gain.reshape(1, model))
 
 
 def solution(mesh):

time: 126 us -> 131 us (1.040)
  the two profiles are of different devices: /device:TPU:20 before, /device:TPU:18 now
where the time goes in v3:
time: 131 us
  Pallas kernels  130 us (99%)
    pallas_call x1, Pallas kernels, on_device(): pl.pallas_call(functools.partial(kernel, n_ctx, n_tp), out_shape=(jax.Sha...  126 us
    pallas_call x1, Pallas kernels, on_device(): pl.pallas_call(scale_rows, grid=(cap // 16,), out_shape=(out, out), in_sp...  3.86 us

profile of v3, /device:TPU:18, one launch (start us, length us, event | category | flops | bytes accessed | tf_op | source)
XLA Modules:
  0.0 130.9 jit_solution(12737348213027287078)
XLA Ops:
  0.6 126.4 %shard_map.95 = (f32[64,8192]{1,0:T(8,128)}, f32[64,128]{1,0:T(8,128)}) custom-call(bf16[256,1024]{1,0:T(8,128)(2,1)} %q_ref.1, bf16[256,256]{1,0:T(8,128)(2,1)} %k_ref.1, bf16[256,256]{1,0:T(8,128)(2,1)} %v_ref.1, s32[8,1,256]{2,1,0:T(1,128)} %bitcast.4, s32[1,256]{1,0:T(1,128)} %bitcast.5, bf16[1024,8192]{1,0:T(8,128)(2,1)} %w_ref.1, bf16[64,8192]{1,0:T(8,128)(2,1)} %res_ref.1), custom_call_target="tpu_custom_call" | custom-call | tf_op jit(solution)/shard_map/pallas_call | solution.py:541
  127.1 3.9 %shard_map.96 = (bf16[64,8192]{1,0:T(8,128)(2,1)}, bf16[64,8192]{1,0:T(8,128)(2,1)}) custom-call(f32[64,8192]{1,0:T(8,128)} %get-tuple-element.4.hidden_ref, f32[64,128]{1,0:T(8,128)} %get-tuple-element.5.inverse_ref, f32[1,8192]{1,0:T(1,128)} %bitcast.3), custom_call_target="tpu_custom_call" | custom-call | tf_op jit(solution)/shard_map/pallas_call | solution.py:584

commit v4 on v3

--- a/solution.py
+++ b/solution.py
@@ -133,11 +133,6 @@
             device_id={"tp": inward},
         )
 
-    @pl.when(at_end)
-    def _():
-        for f in range(FAR_TILES):
-            ship_copy(f).start()
-
     def kv_copies(src, place, send, where):
         dst = pl.ds(place * rows, rows)
         out = []
@@ -177,6 +172,11 @@
     def _():
         for cp in mate_copies():
             cp.start()
+
+    @pl.when(at_end)
+    def _():
+        for f in range(FAR_TILES):
+            ship_copy(f).start()
 
     kbuf[window * rows :, :] = k_ref[...]
     vbuf[window * rows :, :] = v_ref[...]
@@ -404,6 +404,8 @@
             ).astype(jnp.bfloat16)
             cp.start()
 
+    each_tile(functools.partial(pump, 0), 0, near)
+
     @pl.when(helper)
     def _():
         for f in range(FAR_TILES):
@@ -411,7 +413,7 @@
                 spread_copy(r, f).wait_recv()
                 mate_weights(r, f).start()
 
-    each_tile(functools.partial(pump, 0), 0, near)
+    each_tile(functools.partial(pump, 1), 0, near)
 
     @pl.when(helper)
     def _():
@@ -446,7 +448,7 @@
 
             each_tile(far_send_on, near, tiles)
 
-    for j in range(1, n_tp - 1):
+    for j in range(2, n_tp - 1):
         each_tile(functools.partial(pump, j), 0, near)
     for j in range(n_tp - 1):
         each_tile(functools.partial(pump, j), near, tiles)

time: 131 us -> 121 us (0.924)
  the two profiles are of different devices: /device:TPU:18 before, /device:TPU:20 now
where the time goes in v4:
time: 121 us; the launch traced here: 120 us
  Pallas kernels  120 us (99%)
    pallas_call x1, Pallas kernels, on_device(): pl.pallas_call(functools.partial(kernel, n_ctx, n_tp), out_shape=(jax.Sha...  116 us
    pallas_call x1, Pallas kernels, on_device(): pl.pallas_call(scale_rows, grid=(cap // 16,), out_shape=(out, out), in_sp...  3.86 us

profile of v4, /device:TPU:20, one launch (start us, length us, event | category | flops | bytes accessed | tf_op | source)
XLA Modules:
  0.0 120.2 jit_solution(17563040065766190694)
XLA Ops:
  0.6 115.7 %shard_map.95 = (f32[64,8192]{1,0:T(8,128)}, f32[64,128]{1,0:T(8,128)}) custom-call(bf16[256,1024]{1,0:T(8,128)(2,1)} %q_ref.1, bf16[256,256]{1,0:T(8,128)(2,1)} %k_ref.1, bf16[256,256]{1,0:T(8,128)(2,1)} %v_ref.1, s32[8,1,256]{2,1,0:T(1,128)} %bitcast.4, s32[1,256]{1,0:T(1,128)} %bitcast.5, bf16[1024,8192]{1,0:T(8,128)(2,1)} %w_ref.1, bf16[64,8192]{1,0:T(8,128)(2,1)} %res_ref.1), custom_call_target="tpu_custom_call" | custom-call | tf_op jit(solution)/shard_map/pallas_call | solution.py:543
  116.4 3.9 %shard_map.96 = (bf16[64,8192]{1,0:T(8,128)(2,1)}, bf16[64,8192]{1,0:T(8,128)(2,1)}) custom-call(f32[64,8192]{1,0:T(8,128)} %get-tuple-element.4.hidden_ref, f32[64,128]{1,0:T(8,128)} %get-tuple-element.5.inverse_ref, f32[1,8192]{1,0:T(1,128)} %bitcast.3), custom_call_target="tpu_custom_call" | custom-call | tf_op jit(solution)/shard_map/pallas_call | solution.py:586
